TPU v7x, 32 devices: a whole 2x2x4 slice. The times are simulated.
32 devices in a mesh: bin: 8 (over y, x, core), trk: 4 (over z).
Axes of the slice: x: 2, y: 2, z: 4, core: 2. Of those that a mesh axis runs over, the one named last changes fastest.
Arguments:
- trunk: bfloat16 [2048, 1536], P(('bin', 'trk')), may hold values from -6 to 6
- norm_gain: float32 [1536], replicated, may hold values from 0.1 to 1.9
- w_query: bfloat16 [1536, 1024], replicated, may hold values from -0.4375 to 0.4375
- w_kv: bfloat16 [1536, 256], replicated, may hold values from -0.15625 to 0.15625
- w_out: bfloat16 [1024, 1536], replicated, may hold values from -0.1875 to 0.1875
- w_up: bfloat16 [1536, 768], replicated, may hold values from -0.15625 to 0.15625
- skip: bfloat16 [8192, 768], P(('bin', 'trk')), may hold values from -6 to 6
- conv_w: bfloat16 [5, 768, 768], replicated, may hold values from -0.09375 to 0.09375
- head_w: bfloat16 [768, 3072], P(None, 'trk'), may hold values from -0.21875 to 0.21875
- head_bias: float32 [3072], P('trk'), may hold values from -4 to 4
- targets: bfloat16 [8192, 3072], P('bin', 'trk'), may hold values from 0.049804688 to 4
- missing: int32 [2048], P('bin'), may hold values 0 or 1
- group_ids: int32 [3072, 1], replicated, may hold values from 0 to 10
- group_weight: float32 [11], replicated, may hold values from 0.25 to 4
Outputs:
- prediction: bfloat16 [8192, 3072], P('bin', 'trk')
- head_grad: float32 [768, 3072], P('bin', 'trk')
- feature_grad: bfloat16 [8192, 768], P(('bin', 'trk'))
Inputs may be any that keep to these rules, and one draw needn't show every extreme that they name: `group_ids`: every group id is held by at least one track.
All inputs are finite; a program needn't handle non-finite values. No bound on the sum of `missing` on one device may be relied on, other than what follows from the above.
Results may differ from a plain program's by a relative error of at most 0.019.
Values may be sent and summed in bfloat16 or wider, within the bound.
A program may use at most 128 MiB of HBM per device.

v0:
```python
import math

import jax
import jax.numpy as jnp
from jax import lax
from jax.sharding import PartitionSpec as P

logit_cap = 20.0


def padded_2(value, sides, width):
    for axis, dim in sides:
        size, length = (lax.axis_size(axis), value.shape[dim])
        up = [(i, (i + 1) % size) for i in range(size - 1)]
        down = [(j, i) for i, j in up]
        last = lax.slice_in_dim(value, length - width, length, axis=dim)
        initial = lax.slice_in_dim(value, 0, width, axis=dim)
        before = lax.ppermute(last, axis, up)
        after = lax.ppermute(initial, axis, down)
        value = jnp.concatenate([before, value, after], axis=dim)
    return value


def attend_block(state_pair, queries, key_block, value_block, score_scale):
    numerator, denominator = state_pair
    scores = (
        jnp.einsum("rhd,nd->rhn", queries, key_block, preferred_element_type=jnp.float32)
        * score_scale
    )
    scores = logit_cap * jnp.tanh(scores / logit_cap)
    exp_weights = jnp.exp(scores)
    numerator = numerator + jnp.einsum(
        "rhn,nd->rhd",
        exp_weights.astype(jnp.bfloat16),
        value_block,
        preferred_element_type=jnp.float32,
    )
    denominator = denominator + jnp.sum(exp_weights, axis=2)
    return (numerator, denominator)


def make_folder(queries, head_dim):
    score_scale = 1.0 / math.sqrt(head_dim)

    def fold(accum, key_piece, offset):
        piece_rows = key_piece.shape[0]
        block_rows = math.gcd(piece_rows, 2048)
        stacked = key_piece.reshape(piece_rows // block_rows, block_rows, key_piece.shape[1])

        def fold_step(running, one_block):
            updated = attend_block(
                running, queries, one_block[:, :head_dim], one_block[:, head_dim:], score_scale
            )
            return (updated, None)

        result, _ = lax.scan(fold_step, accum, stacked)
        return result

    return fold


def body(
    trunk,
    norm_gain,
    w_query,
    w_kv,
    w_out,
    w_up,
    skip,
    conv_w,
    head_w,
    head_bias,
    targets,
    missing,
    group_ids,
    group_weight,
):
    row_count = trunk.shape[0]
    head_dim = w_kv.shape[1] // 2
    head_count = w_query.shape[1] // head_dim
    widened = trunk.astype(jnp.float32)
    meansq = jnp.mean(widened * widened, axis=1, keepdims=True)
    normed = (widened * lax.rsqrt(meansq + 1e-06) * norm_gain).astype(jnp.bfloat16)
    queries = (
        jnp.dot(normed, w_query, preferred_element_type=jnp.float32)
        .astype(jnp.bfloat16)
        .reshape(row_count, head_count, head_dim)
    )
    keyvals = jnp.dot(normed, w_kv, preferred_element_type=jnp.float32).astype(jnp.bfloat16)
    start_pair = (
        jnp.zeros((row_count, head_count, head_dim), jnp.float32),
        jnp.zeros((row_count, head_count), jnp.float32),
    )
    folder = make_folder(queries, head_dim)
    numerator, denominator = folder(
        start_pair, lax.all_gather(keyvals, ("bin", "trk"), axis=0, tiled=True), jnp.int32(0)
    )
    attended = (
        (numerator / denominator[:, :, None])
        .astype(jnp.bfloat16)
        .reshape(row_count, head_count * head_dim)
    )
    hidden = (widened + jnp.dot(attended, w_out, preferred_element_type=jnp.float32)).astype(
        jnp.bfloat16
    )
    upward = jnp.dot(hidden, w_up, preferred_element_type=jnp.float32)
    factor = skip.shape[0] // row_count
    upsampled = (jnp.repeat(upward, factor, axis=0) + skip.astype(jnp.float32)).astype(jnp.bfloat16)
    tap_count = conv_w.shape[0]
    rim_width = tap_count // 2
    padded = padded_2(upsampled, ((("bin", "trk"), 0),), rim_width)
    pos_count = upsampled.shape[0]
    windows = jnp.concatenate([padded[tap : tap + pos_count] for tap in range(tap_count)], axis=1)
    kernel_flat = conv_w.reshape(tap_count * conv_w.shape[1], conv_w.shape[2])
    conved = jnp.dot(windows, kernel_flat, preferred_element_type=jnp.float32)
    feature = (upsampled.astype(jnp.float32) + jax.nn.gelu(conved)).astype(jnp.bfloat16)
    panel_feat = lax.all_gather(feature, "trk", axis=0, tiled=True)
    logits = jnp.dot(panel_feat, head_w, preferred_element_type=jnp.float32) + head_bias
    smooth = jax.nn.softplus(logits)
    prediction = smooth.astype(jnp.bfloat16)
    tile_width = head_w.shape[1]
    groups = group_weight.shape[0]
    total_tracks = group_ids.shape[0]
    labels = jnp.arange(groups, dtype=jnp.int32)
    counts = jnp.sum((group_ids == labels[None, :]).astype(jnp.int32), axis=0)
    per_group = group_weight * total_tracks / (groups * counts.astype(jnp.float32))
    local_ids = lax.dynamic_slice_in_dim(
        group_ids, lax.axis_index("trk") * tile_width, tile_width, 0
    )
    track_scale = jnp.sum(jnp.where(local_ids == labels[None, :], per_group[None, :], 0.0), axis=1)
    keep_mask = 1.0 - jnp.repeat(missing.astype(jnp.float32), factor)[:, None]
    misfit = smooth - targets.astype(jnp.float32)
    slope_grad = (keep_mask * track_scale[None, :] * misfit * jax.nn.sigmoid(logits)).astype(
        jnp.bfloat16
    )
    positions = panel_feat.shape[0] * lax.axis_size("bin")
    product = lax.dot_general(
        panel_feat, slope_grad, (((0,), (0,)), ((), ())), preferred_element_type=jnp.float32
    )
    head_grad = lax.psum_scatter(
        (product / positions).astype(jnp.bfloat16), "bin", scatter_dimension=0, tiled=True
    ).astype(jnp.float32)
    partial_value = lax.dot_general(
        slope_grad, head_w, (((1,), (1,)), ((), ())), preferred_element_type=jnp.float32
    )
    feature_grad = lax.psum_scatter(
        partial_value.astype(jnp.bfloat16), "trk", scatter_dimension=0, tiled=True
    )
    return (prediction, head_grad, feature_grad)


def solution(mesh):
    in_specs = (
        P(("bin", "trk"), None),
        P(),
        P(),
        P(),
        P(),
        P(),
        P(("bin", "trk"), None),
        P(),
        P(None, "trk"),
        P("trk"),
        P("bin", "trk"),
        P("bin"),
        P(),
        P(),
    )
    out_specs = (P("bin", "trk"), P("bin", "trk"), P(("bin", "trk"), None))
    return jax.shard_map(body, mesh=mesh, in_specs=in_specs, out_specs=out_specs, check_vma=False)
```

profile of v0, /device:TPU:14, one launch (start us, length us, event | category | flops | bytes accessed | tf_op | source)
XLA Modules:
  0.0 223.3 jit_solution(8958994364499204388)
XLA Ops:
  7.2 0.0 copy-start
  7.2 0.0 all-gather.3.cloned.1.call-start
  7.2 1.2 fusion.26
  8.5 2.2 convolution_convert_fusion.2
  10.6 0.0 all-gather.3.cloned.1.call-update
  10.7 0.0 all-gather.5.cloned.1.call-start
  10.7 0.0 copy-done
  10.7 1.6 fusion.11
  12.4 53.3 %all-gather.3.cloned.1.call-done = bf16[2048,256]{1,0:T(8,128)(2,1)} async-done(((bf16[64,256]{1,0:T(8,128)(2,1)}), bf16[2048,256]{1,0:T(8,128)(2,1)}) %all-gather.3.cloned.1.call-update) | async-done | bytes 1048592 | tf_op jit(solution)/shard_map/all_gather | solution.py:96
  65.7 0.0 copy-start.5
  65.7 2.5 %fusion.38 = (f32[64,8]{1,0:T(8,128)S(1)}, bf16[64,8,2048]{2,1,0:T(8,128)(2,1)S(1)}) fusion(bf16[64,8,128]{2,1,0:T(8,128)(2,1)S(1)} %bitcast.33, bf16[2048,256]{1,0:T(8,128)(2,1)} %all-gather.3.cloned.1.call-done), kind=kOutput, calls=%fused_computation.59 | convolution fusion | flops 272629248 | bytes 2754560 | tf_op jit(solution)/shard_map/while/body/eval_jaxpr/rhd,nd->rhn/dot_general | solution.py:27
  68.2 0.0 copy-start.1
  68.2 0.0 copy-done.5
  68.2 1.4 fusion.7
  69.6 0.0 copy-done.1
  69.6 3.8 %fusion.10 = f32[64,768]{1,0:T(8,128)S(1)} fusion(bf16[1536,768]{1,0:T(8,128)(2,1)} %param.19, bf16[1024,1536]{1,0:T(8,128)(2,1)} %param.18, bf16[64,1536]{1,0:T(8,128)(2,1)S(1)} %copy-done.1, bf16[8,8,8,128]{3,2,1,0:T(8,128)(2,1)} %bitcast.32), kind=kOutput, calls=%fused_computation.13 | convolution fusion | flops 352616448 | bytes 6029312 | tf_op jit(solution)/shard_map/dot_general | solution.py:106
  73.3 1.0 broadcast_in_dim.12
  74.4 2.3 %reshape.45 = f32[256,768]{1,0:T(8,128)} reshape(f32[64,4,768]{2,1,0:T(4,128)} %broadcast_in_dim.12) | data formatting | bytes 1572864 | tf_op jit(solution)/shard_map/reshape | solution.py:108
  76.7 1.3 add_convert_fusion
  78.0 2.6 %collective-permute-start = (bf16[2,768]{1,0:T(2,128)(2,1)S(1)}, bf16[2,768]{1,0:T(2,128)(2,1)S(1)}, u32[]{:S(2)}, u32[]{:S(2)}) collective-permute-start(bf16[2,768]{1,0:T(2,128)(2,1)S(1)} %get-tuple-element.21), channel_id=1, source_target_pairs={{0,1},{1,2},{2,3},{3,4},{4,5},{5,6},{6,7},{7,8},{8,9},{9,10},{10,1... | collective-permute-start | bytes 9224 | tf_op jit(solution)/shard_map/ppermute | solution.py:18
  80.6 3.2 %collective-permute-start.1 = (bf16[2,768]{1,0:T(2,128)(2,1)S(1)}, bf16[2,768]{1,0:T(2,128)(2,1)S(1)}, u32[]{:S(2)}, u32[]{:S(2)}) collective-permute-start(bf16[2,768]{1,0:T(2,128)(2,1)S(1)} %get-tuple-element.20), channel_id=1, source_target_pairs={{1,0},{2,1},{3,2},{4,3},{5,4},{6,5},{7,6},{8,7},{9,8},{10,9},{11,1... | collective-permute-start | bytes 9224 | tf_op jit(solution)/shard_map/ppermute | solution.py:19
  83.8 0.0 collective-permute-done
  83.9 0.1 fusion.25
  84.0 0.1 fusion.30
  84.1 2.0 collective-permute-done.1
  86.1 0.1 fusion.23
  86.2 0.1 fusion.29
  86.3 0.0 copy-start.3
  86.3 0.0 copy-start.2
  86.3 0.0 copy-start.7
  86.3 0.0 copy-start.6
  86.3 5.3 %fusion.20 = bf16[256,768]{1,0:T(8,128)(2,1)} fusion(bf16[256,768]{1,0:T(8,128)(2,1)S(1)} %add_convert_fusion, bf16[256,3840]{1,0:T(8,128)(2,1)S(1)} %fusion.29, bf16[3840,768]{1,0:T(8,128)(2,1)} %bitcast.35), kind=kOutput, calls=%fused_computation.25 | convolution fusion | flops 1512112128 | bytes 8650752 | tf_op jit(solution)/shard_map/dot_general | solution.py:115
  91.6 0.0 all-gather.5.cloned.1.call-update
  91.6 0.0 reduce-scatter.3.cloned.1.call-start
  91.7 0.0 copy-done.3
  91.7 0.1 broadcast_in_dim.13
  91.8 0.1 sub.20
  91.9 0.0 copy-done.2
  92.0 0.1 convert_reduce_fusion
  92.1 0.0 copy-done.7
  92.1 0.1 select_reduce_fusion
  92.2 39.9 %all-gather.5.cloned.1.call-done = bf16[1024,768]{1,0:T(8,128)(2,1)} async-done(((bf16[256,768]{1,0:T(8,128)(2,1)}), bf16[1024,768]{1,0:T(8,128)(2,1)}) %all-gather.5.cloned.1.call-update) | async-done | bytes 1572880 | tf_op jit(solution)/shard_map/all_gather | solution.py:117
  132.1 0.0 copy-done.6
  132.2 0.0 copy-start.4
  132.2 7.0 %multiply_convert_fusion = (bf16[1024,768]{1,0:T(8,128)(2,1)S(1)}, bf16[1024,768]{1,0:T(8,128)(2,1)}) fusion(bf16[1024,768]{1,0:T(8,128)(2,1)} %param.24, f32[768]{0:T(1024)S(1)} %select_reduce_fusion, f32[1024]{0:T(1024)S(1)} %sub.20, f32[768]{0:T(1024)S(1)} %copy-done.6, bf16[1024,768]{1,0:T(8,128)(2,1)} %all-gather.5.cloned.1.call-done, ...), kind=kOutput, calls=%fused_computation.2 | convolution fusion | flops 1221328896 | bytes 7481344 | tf_op jit(solution)/shard_map/dot_general | solution.py:118
  139.1 0.0 copy-start.8
  139.1 1.2 copy-done.8
  140.3 0.0 copy-done.4
  140.3 2.5 %multiply_convert_fusion.1 = bf16[768,768]{1,0:T(8,128)(2,1)} fusion(bf16[1024,768]{1,0:T(8,128)(2,1)S(1)} %copy-done.4, bf16[1024,768]{1,0:T(8,128)(2,1)S(1)} %get-tuple-element.13), kind=kOutput, calls=%fused_computation.4 | convolution fusion | flops 1209139200 | bytes 4325376 | tf_op jit(solution)/shard_map/dot_general | solution.py:137
  142.8 0.0 reduce-scatter.3.cloned.1.call-update
  142.8 0.0 reduce-scatter.5.cloned.1.call-start
  142.9 4.3 %convolution_convert_fusion = bf16[1024,768]{1,0:T(8,128)(2,1)} fusion(bf16[1024,768]{1,0:T(8,128)(2,1)} %copy-done.8, bf16[768,768]{1,0:T(8,128)(2,1)} %param.22), kind=kOutput, calls=%fused_computation.9 | convolution fusion | flops 1208745984 | bytes 4325376 | tf_op jit(solution)/shard_map/dot_general | solution.py:143
  147.2 0.0 reduce-scatter.5.cloned.1.call-update
  147.2 31.5 %reduce-scatter.3.cloned.1.call-done = bf16[96,768]{1,0:T(8,128)(2,1)} async-done(((bf16[768,768]{1,0:T(8,128)(2,1)}), bf16[96,768]{1,0:T(8,128)(2,1)}) %reduce-scatter.3.cloned.1.call-update) | async-done | bytes 147472 | tf_op jit(solution)/shard_map/reduce_scatter | solution.py:140
  178.7 1.6 convert_element_type.79
  180.4 36.3 %reduce-scatter.5.cloned.1.call-done = bf16[256,768]{1,0:T(8,128)(2,1)} async-done(((bf16[1024,768]{1,0:T(8,128)(2,1)}), bf16[256,768]{1,0:T(8,128)(2,1)}) %reduce-scatter.5.cloned.1.call-update) | async-done | bytes 393232 | tf_op jit(solution)/shard_map/reduce_scatter | solution.py:146
  (7 shorter events, 0.1 us)
Async XLA Ops:
  7.2 3.6 %copy-start = (bf16[1536,1024]{1,0:T(8,128)(2,1)S(1)}, bf16[1536,1024]{1,0:T(8,128)(2,1)}, u32[]{:S(2)}) copy-start(bf16[1536,1024]{1,0:T(8,128)(2,1)} %param.16) | copy-start | bytes 9437188
  7.2 58.5 %all-gather.3.cloned.1.call-start = ((), (), s32[]{:S(2)}) async-start(), calls=%async_computation.2 | async-start | bytes 1081344 | tf_op jit(solution)/shard_map/all_gather | solution.py:96
  10.7 121.5 %all-gather.5.cloned.1.call-start = ((), (), s32[]{:S(2)}) async-start(), calls=%async_computation.3 | async-start | bytes 1966080 | tf_op jit(solution)/shard_map/all_gather | solution.py:117
  65.7 2.5 %copy-start.5 = (bf16[2048,256]{1,0:T(8,128)(2,1)S(1)}, bf16[2048,256]{1,0:T(8,128)(2,1)}, u32[]{:S(2)}) copy-start(bf16[2048,256]{1,0:T(8,128)(2,1)} %all-gather.3.cloned.1.call-done) | copy-start | bytes 3145732
  68.2 1.4 copy-start.1
  78.0 5.9 %collective-permute-start = (bf16[2,768]{1,0:T(2,128)(2,1)S(1)}, bf16[2,768]{1,0:T(2,128)(2,1)S(1)}, u32[]{:S(2)}, u32[]{:S(2)}) collective-permute-start(bf16[2,768]{1,0:T(2,128)(2,1)S(1)} %get-tuple-element.21), channel_id=1, source_target_pairs={{0,1},{1,2},{2,3},{3,4},{4,5},{5,6},{6,7},{7,8},{8,9},{9,10},{10,1... | collective-permute-start | bytes 9224 | tf_op jit(solution)/shard_map/ppermute | solution.py:18
  80.6 5.5 %collective-permute-start.1 = (bf16[2,768]{1,0:T(2,128)(2,1)S(1)}, bf16[2,768]{1,0:T(2,128)(2,1)S(1)}, u32[]{:S(2)}, u32[]{:S(2)}) collective-permute-start(bf16[2,768]{1,0:T(2,128)(2,1)S(1)} %get-tuple-element.20), channel_id=1, source_target_pairs={{1,0},{2,1},{3,2},{4,3},{5,4},{6,5},{7,6},{8,7},{9,8},{10,9},{11,1... | collective-permute-start | bytes 9224 | tf_op jit(solution)/shard_map/ppermute | solution.py:19
  86.3 5.4 %copy-start.3 = (s32[256]{0:T(256)S(1)}, s32[256]{0:T(256)}, u32[]{:S(2)}) copy-start(s32[256]{0:T(256)} %param.25) | copy-start | bytes 3076
  86.3 5.6 %copy-start.2 = (s32[3072,1]{0,1:T(1,128)S(1)}, s32[3072,1]{0,1:T(1,128)}, u32[]{:S(2)}) copy-start(s32[3072,1]{0,1:T(1,128)} %param.26) | copy-start | bytes 36868
  86.3 5.8 %copy-start.7 = (f32[11]{0:T(128)S(1)}, f32[11]{0:T(128)}, u32[]{:S(2)}) copy-start(f32[11]{0:T(128)} %param.27) | copy-start | bytes 136
  86.3 45.8 %copy-start.6 = (f32[768]{0:T(1024)S(1)}, f32[768]{0:T(1024)}, u32[]{:S(2)}) copy-start(f32[768]{0:T(1024)} %param.23) | copy-start | bytes 9220
  91.6 87.1 %reduce-scatter.3.cloned.1.call-start = ((), (), s32[]{:S(2)}) async-start(), calls=%async_computation.4 | async-start | bytes 1327104 | tf_op jit(solution)/shard_map/reduce_scatter | solution.py:140
  132.2 8.2 %copy-start.4 = (bf16[1024,768]{1,0:T(8,128)(2,1)S(1)}, bf16[1024,768]{1,0:T(8,128)(2,1)}, u32[]{:S(2)}) copy-start(bf16[1024,768]{1,0:T(8,128)(2,1)} %all-gather.5.cloned.1.call-done) | copy-start | bytes 4718596
  139.1 1.2 copy-start.8
  142.8 73.9 %reduce-scatter.5.cloned.1.call-start = ((), (), s32[]{:S(2)}) async-start(), calls=%async_computation.5 | async-start | bytes 1966080 | tf_op jit(solution)/shard_map/reduce_scatter | solution.py:146
Sparse Core Ops, SparseCore 0:
  11.6 54.0 all-gather.2
  91.8 40.3 all-gather.4
  143.0 35.7 reduce-scatter.2
  181.6 35.1 reduce-scatter.4
where the time goes:
time: 226 us; the launch traced here: 223 us
  waiting for transfers between devices  163 us (72%)
  matrix products  30.6 us (14%)
  between operations  14 us (6%)
  starting transfers between devices  6.01 us (3%)
  local copies, waits for them, and re-layouts  4.8 us (2%)
  other arithmetic  4.79 us (2%)
    all_gather x1, waiting for transfers between devices, body(): lax.all_gather(keyvals, ('bin', 'trk'), axis=0, tiled=True)  53.3 us
    all_gather x1, waiting for transfers between devices, body(): panel_feat = lax.all_gather(feature, 'trk', axis=0, tiled=True)  39.9 us
    reduce_scatter x1, waiting for transfers between devices, body(): lax.psum_scatter(partial_value.astype(jnp.bfloat16), 'trk', scatter_dimen...  36.3 us
    reduce_scatter x1, waiting for transfers between devices, body(): lax.psum_scatter((product / positions).astype(jnp.bfloat16), 'bin', scatt...  31.5 us
    dot_general x1, matrix products, body(): jnp.dot(panel_feat, head_w, preferred_element_type=jnp.float32) + head_bias  6.99 us
    dot_general x1, matrix products, body(): conved = jnp.dot(windows, kernel_flat, preferred_element_type=jnp.float32)  5.29 us
  transfers between devices with their start and end apart: 6, of which 5 were waited for; matrix products, arithmetic and copies ran while one was open for 4% of the time, Pallas kernels for 0%

commit v1 on v0

v1 whole, which is shorter than its diff:
```python
import functools
import math

import jax
import jax.numpy as jnp
from jax import lax
from jax.experimental import pallas as pl
from jax.experimental.pallas import tpu as pltpu
from jax.sharding import PartitionSpec as P

CAP = 20.0
F32 = jnp.float32
BF16 = jnp.bfloat16
NT = (((1,), (1,)), ((), ()))
TN = (((0,), (0,)), ((), ()))


def xor(x, y, size):
    out, bit = 0, 1
    while bit < size:
        a = lax.rem(lax.div(x, bit), 2)
        if isinstance(y, int):
            if (y // bit) % 2:
                a = 1 - a
        else:
            c = lax.rem(lax.div(y, bit), 2)
            a = a + c - 2 * a * c
        out = out + a * bit
        bit *= 2
    return out


def dot(a, b):
    return jnp.dot(a, b, preferred_element_type=F32)


def kernel(
    nb, nt, positions,
    trunk, gain, bias, scale, missing,
    wq, wkv, wout, wup, skip, convw, headw, targets,
    pred, hgrad, fgrad,
    wq_v, wkv_v, wout_v, wup_v, conv_v, head_v, targ_v,
    skip_all, kv_all, q_v, acc_v, den_v, norm_v, hid_v, up_all, u32, win, xs, feat, slope,
    part, part_in, hg, hg_in, hs, hs_in,
    load_sem, pred_sem,
    skip_s, skip_r, kv1_s, kv1_r, kv2_s, kv2_r, kv3_s, kv3_r, up_s, up_r,
    halo_s, halo_r, part_s, part_r, hg_s, hg_r, hs_s, hs_r,
):
    b, t = lax.axis_index("bin"), lax.axis_index("trk")
    rows, chan = trunk.shape
    dk = wkv.shape[1] // 2
    heads = wq.shape[1] // dk
    npos, c2 = skip.shape
    tracks = headw.shape[1]
    taps = convw.shape[0]
    rim = taps // 2
    factor = npos // rows
    group = nt * npos
    half = nb // 2
    tile = 256

    def send(src, dst, ssem, rsem, bb, tt):
        return pltpu.make_async_remote_copy(
            src_ref=src, dst_ref=dst, send_sem=ssem, recv_sem=rsem,
            device_id=(bb, tt), device_id_type=pl.DeviceIdType.MESH,
        )

    loads = [
        pltpu.make_async_copy(src, dst, load_sem.at[i])
        for i, (src, dst) in enumerate([
            (wkv, wkv_v), (wq, wq_v), (wout, wout_v), (wup, wup_v),
            (skip, skip_all.at[t]), (convw, conv_v), (headw, head_v), (targets, targ_v),
        ])
    ]
    for load in loads:
        load.start()

    barrier = pltpu.get_barrier_semaphore()
    greet = [(b, xor(t, o, nt)) for o in range(1, nt)]
    greet += [(xor(b, 2 * j, nb), t) for j in range(1, half)]
    greet += [(lax.rem(b + 1, nb), t), (lax.rem(b + nb - 1, nb), t)]
    for dev in greet:
        pl.semaphore_signal(barrier, inc=1, device_id=dev, device_id_type=pl.DeviceIdType.MESH)
    pl.semaphore_wait(barrier, len(greet))

    core = xor(b, 1, nb)
    skip_c = [
        send(skip, skip_all.at[t], skip_s.at[o], skip_r.at[o], b, xor(t, o, nt)) for o in range(1, nt)
    ]
    for copy in skip_c:
        copy.start()

    wide = trunk[...].astype(F32)
    meansq = jnp.mean(wide * wide, axis=1, keepdims=True)
    norm_v[...] = (wide * lax.rsqrt(meansq + 1e-06) * gain[...]).astype(BF16)
    loads[0].wait()
    kv_all[b, t] = dot(norm_v[...], wkv_v[...]).astype(BF16)
    kv1 = [
        send(kv_all.at[b, t], kv_all.at[b, t], kv1_s.at[o], kv1_r.at[o], b, xor(t, o, nt))
        for o in range(1, nt)
    ]
    for copy in kv1:
        copy.start()

    loads[1].wait()
    per = tile // dk
    for i in range(heads // per):
        res = dot(norm_v[...], wq_v[:, i * tile:(i + 1) * tile]).astype(BF16)
        for k in range(per):
            h = i * per + k
            q_v[h * rows:(h + 1) * rows, :] = res[:, k * dk:(k + 1) * dk]

    for copy in kv1:
        copy.wait_recv()
    kv2 = [
        send(kv_all.at[b], kv_all.at[b], kv2_s.at[j], kv2_r.at[j], xor(b, 2 * j, nb), t)
        for j in range(1, half)
    ]
    for copy in kv2:
        copy.start()
    kv3 = []
    for j in range(half):
        if j:
            kv2[j - 1].wait_recv()
        g = xor(b, 2 * j, nb)
        copy = send(kv_all.at[g], kv_all.at[g], kv3_s.at[j], kv3_r.at[j], core, t)
        copy.start()
        kv3.append(copy)

    acc_v[...] = jnp.zeros_like(acc_v)
    den_v[...] = jnp.zeros_like(den_v)
    score_scale = 1.0 / math.sqrt(dk)

    def fold(g):
        kv = kv_all[g].reshape(nt * rows, 2 * dk)
        s = lax.dot_general(q_v[...], kv[:, :dk], NT, preferred_element_type=F32)
        e = jnp.exp(CAP * jnp.tanh(s * (score_scale / CAP)))
        acc_v[...] += dot(e.astype(BF16), kv[:, dk:])
        d = e[:, :dk]
        for k in range(1, nt * rows // dk):
            d = d + e[:, k * dk:(k + 1) * dk]
        den_v[...] += d

    def fold_own(j, carry):
        fold(xor(b, 2 * j, nb))
        return carry

    def fold_core(j, carry):
        fold(xor(core, 2 * j, nb))
        return carry

    lax.fori_loop(0, half, fold_own, 0)
    for copy in kv3:
        copy.wait_recv()
    lax.fori_loop(0, half, fold_core, 0)

    att = (acc_v[...] / jnp.sum(den_v[...], axis=1, keepdims=True)).astype(BF16)
    for h in range(heads):
        norm_v[:, h * dk:(h + 1) * dk] = att[h * rows:(h + 1) * rows, :]
    loads[2].wait()
    for i in range(chan // tile):
        cols = slice(i * tile, (i + 1) * tile)
        hid_v[:, cols] = (
            trunk[:, cols].astype(F32) + dot(norm_v[:, :heads * dk], wout_v[:, cols])
        ).astype(BF16)
    loads[3].wait()
    for i in range(c2 // tile):
        cols = slice(i * tile, (i + 1) * tile)
        up_all[t, :, cols] = dot(hid_v[...], wup_v[:, cols]).astype(BF16)
    ups = [
        send(up_all.at[t], up_all.at[t], up_s.at[o], up_r.at[o], b, xor(t, o, nt)) for o in range(1, nt)
    ]
    for copy in ups:
        copy.start()

    loads[4].wait()
    for copy in skip_c:
        copy.wait_recv()
    for copy in ups:
        copy.wait_recv()
    spread = (
        lax.broadcasted_iota(jnp.int32, (npos, rows), 0) // factor
        == lax.broadcasted_iota(jnp.int32, (npos, rows), 1)
    ).astype(F32).astype(BF16)

    def assemble(c, carry):
        u = (dot(spread, up_all[c]) + skip_all[c].astype(F32)).astype(BF16).astype(F32)
        u32[pl.ds(pl.multiple_of(8 + c * npos, 8), npos), :] = u
        return carry

    lax.fori_loop(0, nt, assemble, 0)
    to_next = send(
        u32.at[pl.ds(group, 8)], u32.at[pl.ds(0, 8)], halo_s.at[0], halo_r.at[0], lax.rem(b + 1, nb), t
    )
    to_prev = send(
        u32.at[pl.ds(8, 8)], u32.at[pl.ds(8 + group, 8)], halo_s.at[1], halo_r.at[1],
        lax.rem(b + nb - 1, nb), t,
    )
    zeros = jnp.zeros((8, c2), F32)

    @pl.when(b < nb - 1)
    def _():
        to_next.start()

    @pl.when(b > 0)
    def _():
        to_prev.start()

    @pl.when(b == 0)
    def _():
        u32[0:8, :] = zeros

    @pl.when(b == nb - 1)
    def _():
        u32[8 + group:16 + group, :] = zeros

    @pl.when(b > 0)
    def _():
        to_next.wait_recv()

    @pl.when(b < nb - 1)
    def _():
        to_prev.wait_recv()

    for i in range(5, 8):
        loads[i].wait()

    def head_step(i, carry):
        o = nt - 1 - i
        c = xor(t, o, nt)
        base = pl.multiple_of(c * npos, npos)
        win[...] = u32[pl.ds(base, npos + 16), :]
        for k in range(taps):
            xs[k] = win[8 + k - rim:8 + k - rim + npos, :].astype(BF16)
        for n in range(c2 // tile):
            cols = slice(n * tile, (n + 1) * tile)
            acc = dot(xs[0], conv_v[0, :, cols])
            for k in range(1, taps):
                acc = acc + dot(xs[k], conv_v[k, :, cols])
            gelu = 0.5 * acc * (1.0 + jnp.tanh(math.sqrt(2.0 / math.pi) * (acc + 0.044715 * acc * acc * acc)))
            feat[pl.ds(base, npos), cols] = (
                u32[pl.ds(pl.multiple_of(base + 8, 8), npos), cols] + gelu
            ).astype(BF16)
        f = feat[pl.ds(base, npos), :]
        span = missing.shape[1]
        pick = (
            (lax.broadcasted_iota(jnp.int32, (npos, span), 0) + base) // factor
            == lax.broadcasted_iota(jnp.int32, (npos, span), 1)
        ).astype(F32).astype(BF16)
        keep_row = (1 - missing[...]).astype(F32).astype(BF16)
        keep = lax.dot_general(
            pick, jnp.broadcast_to(keep_row, (128, span)), NT, preferred_element_type=F32
        )
        keep = jnp.concatenate([keep] * (tile // 128), axis=1)
        for n in range(tracks // tile):
            cols = slice(n * tile, (n + 1) * tile)
            x = dot(f, head_v[:, cols]) + bias[:, cols]
            e = jnp.exp(-jnp.abs(x))
            u = 1.0 + e
            r = 1.0 / u
            smooth = jnp.maximum(x, 0.0) + (jnp.log(u) + (e - (u - 1.0)) * r)
            sig = jnp.where(x >= 0, r, e * r)
            misfit = smooth - targ_v[pl.ds(base, npos), cols].astype(F32)
            slope[pl.ds(base, npos), cols] = (keep * scale[:, cols] * misfit * sig).astype(BF16)
            targ_v[pl.ds(base, npos), cols] = smooth.astype(BF16)
        pltpu.make_async_copy(
            targ_v.at[pl.ds(base, npos)], pred.at[pl.ds(base, npos)], pred_sem.at[i]
        ).start()
        g = slope[pl.ds(base, npos), :]
        for n in range(c2 // tile):
            cols = slice(n * tile, (n + 1) * tile)
            part[o, :, cols] = lax.dot_general(
                g, head_v[cols, :], NT, preferred_element_type=F32
            ).astype(BF16)

        @pl.when(o > 0)
        def _():
            send(part.at[o], part_in.at[o], part_s.at[o], part_r.at[o], b, c).start()

        return carry

    lax.fori_loop(0, nt, head_step, 0)

    block = c2 // nb
    for n in range(c2 // tile):
        rws = slice(n * tile, (n + 1) * tile)
        for m in range(tracks // tile):
            cols = slice(m * tile, (m + 1) * tile)
            hg[rws, cols] = (
                lax.dot_general(feat[:, rws], slope[:, cols], TN, preferred_element_type=F32)
                * (1.0 / positions)
            ).astype(BF16)
    mine = lax.div(b, 2)
    odd = lax.rem(b, 2)
    hgs = []
    for j in range(half):
        row = pl.multiple_of((2 * j + 1 - odd) * block, block)
        copy = send(hg.at[pl.ds(row, block)], hg_in.at[j], hg_s.at[j], hg_r.at[j], core, t)
        copy.start()
        hgs.append(copy)
    for copy in hgs:
        copy.wait_recv()
    hss = []
    for j in range(1, half):
        q = xor(b, 2 * j, nb)
        row = pl.multiple_of(q * block, block)
        hs[j] = (hg[pl.ds(row, block), :].astype(F32) + hg_in[lax.div(q, 2)].astype(F32)).astype(BF16)
        copy = send(hs.at[j], hs_in.at[j], hs_s.at[j], hs_r.at[j], q, t)
        copy.start()
        hss.append(copy)
    own = hg[pl.ds(pl.multiple_of(b * block, block), block), :].astype(F32) + hg_in[mine].astype(F32)
    for j in range(1, half):
        hss[j - 1].wait_recv()
        own = own + hs_in[j].astype(F32)
    hgrad[...] = own

    total = part[0].astype(F32)
    for o in range(1, nt):
        send(part.at[o], part_in.at[o], part_s.at[o], part_r.at[o], b, xor(t, o, nt)).wait_recv()
        total = total + part_in[o].astype(F32)
    fgrad[...] = total.astype(BF16)

    for o in range(1, nt):
        send(part.at[o], part_in.at[o], part_s.at[o], part_r.at[o], b, xor(t, o, nt)).wait_send()
    for copy in skip_c + kv1 + kv2 + kv3 + ups + hgs + hss:
        copy.wait_send()

    @pl.when(b < nb - 1)
    def _():
        to_next.wait_send()

    @pl.when(b > 0)
    def _():
        to_prev.wait_send()

    for i in range(nt):
        base = pl.multiple_of(xor(t, nt - 1 - i, nt) * npos, npos)
        pltpu.make_async_copy(
            targ_v.at[pl.ds(base, npos)], pred.at[pl.ds(base, npos)], pred_sem.at[i]
        ).wait()


def body(
    trunk, norm_gain, w_query, w_kv, w_out, w_up, skip, conv_w,
    head_w, head_bias, targets, missing, group_ids, group_weight,
):
    nb, nt = lax.axis_size("bin"), lax.axis_size("trk")
    rows, chan = trunk.shape
    npos, c2 = skip.shape
    tracks = head_w.shape[1]
    dk = w_kv.shape[1] // 2
    heads = w_query.shape[1] // dk
    taps = conv_w.shape[0]
    group = nt * npos
    half = nb // 2
    block = c2 // nb

    groups = group_weight.shape[0]
    total_tracks = group_ids.shape[0]
    labels = jnp.arange(groups, dtype=jnp.int32)
    counts = jnp.sum((group_ids == labels[None, :]).astype(jnp.int32), axis=0)
    per_group = group_weight * total_tracks / (groups * counts.astype(F32))
    local_ids = lax.dynamic_slice_in_dim(group_ids, lax.axis_index("trk") * tracks, tracks, 0)
    track_scale = jnp.sum(jnp.where(local_ids == labels[None, :], per_group[None, :], 0.0), axis=1)

    vm = pl.BlockSpec(memory_space=pltpu.VMEM)
    hbm = pl.BlockSpec(memory_space=pl.ANY)
    V = pltpu.VMEM
    dma = pltpu.SemaphoreType.DMA
    flops = 2 * (
        rows * chan * (heads + 2) * dk + rows * heads * nb * nt * rows * 2 * dk
        + rows * heads * dk * chan + rows * chan * c2 + group * taps * c2 * c2 + 3 * group * c2 * tracks
    )
    return pl.pallas_call(
        functools.partial(kernel, nb, nt, float(group * nb)),
        out_shape=(
            jax.ShapeDtypeStruct((group, tracks), BF16),
            jax.ShapeDtypeStruct((block, tracks), F32),
            jax.ShapeDtypeStruct((npos, c2), BF16),
        ),
        in_specs=[vm] * 5 + [hbm] * 8,
        out_specs=(hbm, vm, vm),
        scratch_shapes=[
            V(w_query.shape, BF16), V(w_kv.shape, BF16), V(w_out.shape, BF16), V(w_up.shape, BF16),
            V(conv_w.shape, BF16), V(head_w.shape, BF16), V((group, tracks), BF16),
            V((nt, npos, c2), BF16), V((nb, nt, rows, 2 * dk), BF16), V((heads * rows, dk), BF16),
            V((heads * rows, dk), F32), V((heads * rows, dk), F32), V((rows, chan), BF16),
            V((rows, chan), BF16), V((nt, rows, c2), BF16), V((group + 16, c2), F32), V((npos + 16, c2), F32),
            V((taps, npos, c2), BF16), V((group, c2), BF16), V((group, tracks), BF16),
            V((nt, npos, c2), BF16), V((nt, npos, c2), BF16), V((c2, tracks), BF16),
            V((half, block, tracks), BF16), V((half, block, tracks), BF16), V((half, block, tracks), BF16),
            dma((8,)), dma((nt,)),
            dma((nt,)), dma((nt,)), dma((nt,)), dma((nt,)), dma((half,)), dma((half,)),
            dma((half,)), dma((half,)), dma((nt,)), dma((nt,)),
            dma((2,)), dma((2,)), dma((nt,)), dma((nt,)), dma((half,)), dma((half,)),
            dma((half,)), dma((half,)),
        ],
        compiler_params=pltpu.CompilerParams(
            collective_id=0, has_side_effects=True, vmem_limit_bytes=60 * 1024 * 1024
        ),
        cost_estimate=pl.CostEstimate(
            flops=flops, bytes_accessed=24 * 1024 * 1024, transcendentals=4 * 1024 * 1024
        ),
    )(
        trunk, norm_gain[None, :], head_bias[None, :], track_scale[None, :], missing[None, :],
        w_query, w_kv, w_out, w_up, skip, conv_w, head_w, targets,
    )


def solution(mesh):
    in_specs = (
        P(("bin", "trk"), None), P(), P(), P(), P(), P(), P(("bin", "trk"), None), P(),
        P(None, "trk"), P("trk"), P("bin", "trk"), P("bin"), P(), P(),
    )
    out_specs = (P("bin", "trk"), P("bin", "trk"), P(("bin", "trk"), None))
    return jax.shard_map(body, mesh=mesh, in_specs=in_specs, out_specs=out_specs, check_vma=False)
```

time: 226 us -> 119 us (0.53)
  the two profiles are of different devices: /device:TPU:14 before, /device:TPU:0 now
where the time goes in v1:
time: 119 us
  Pallas kernels  109 us (92%)
  local copies, waits for them, and re-layouts  8.02 us (7%)
  other arithmetic  1.59 us (1%)
    pallas_call x1, Pallas kernels, body(): pl.pallas_call(functools.partial(kernel, nb, nt, float(group * nb)), out_...  109 us
    unnamed x7, local copies, waits for them, and re-layouts  4.18 us

profile of v1, /device:TPU:0, one launch (start us, length us, event | category | flops | bytes accessed | tf_op | source)
XLA Modules:
  0.0 119.0 jit_solution(2153130608996358503)
XLA Ops:
  0.6 0.8 convert_reduce_fusion
  1.5 0.7 multiply_divide_fusion
  2.1 1.3 %broadcast_in_dim.28.bias = f32[1,768]{1,0:T(1,128)} reshape(f32[768]{0:T(1024)} %param.23) | data formatting | bytes 6144 | tf_op jit(solution)/shard_map/broadcast_in_dim | solution.py:405
  3.4 0.7 dynamic-slice_reduce_fusion
  4.1 0.1 select_reduce_fusion
  4.2 0.6 broadcast_in_dim.31.scale
  4.8 1.3 %broadcast_in_dim.27.gain = f32[1,1536]{1,0:T(1,128)} reshape(f32[1536]{0:T(1024)} %param.15) | data formatting | bytes 12288 | tf_op jit(solution)/shard_map/broadcast_in_dim | solution.py:405
  6.1 108.7 %shard_map.157 = (bf16[1024,768]{1,0:T(8,128)(2,1)}, f32[96,768]{1,0:T(8,128)}, bf16[256,768]{1,0:T(8,128)(2,1)}) custom-call(bf16[64,1536]{1,0:T(8,128)(2,1)} %trunk.1, f32[1,1536]{1,0:T(1,128)} %broadcast_in_dim.27.gain, f32[1,768]{1,0:T(1,128)} %broadcast_in_dim.28.bias, f32[1,768]{1,0:T(1,128)} %broadcast_in_dim.31.scale, s32[1,256]{1,0:T(1,128)} %bitcast.3, ...), custom_call_target="tpu_custom_call" | custom-call | flops 10804527104 | bytes 25165824 | tf_op jit(solution)/shard_map/pallas_call | solution.py:374
  114.8 0.0 copy-start.1
  114.8 0.0 copy-start
  114.8 2.7 %copy.20 = bf16[1024,768]{1,0:T(8,128)(2,1)} copy(bf16[1024,768]{1,0:T(8,128)(2,1)} %get-tuple-element.6) | data formatting | bytes 3145728
  117.5 0.0 copy-done.1
  117.5 0.7 copy.21
  118.3 0.0 copy-done
  118.3 0.7 copy.22
Async XLA Ops:
  114.8 2.7 %copy-start.1 = (f32[96,768]{1,0:T(8,128)S(1)}, f32[96,768]{1,0:T(8,128)}, u32[]{:S(2)}) copy-start(f32[96,768]{1,0:T(8,128)} %get-tuple-element.7) | copy-start | bytes 884740
  114.8 3.4 %copy-start = (bf16[256,768]{1,0:T(8,128)(2,1)S(1)}, bf16[256,768]{1,0:T(8,128)(2,1)}, u32[]{:S(2)}) copy-start(bf16[256,768]{1,0:T(8,128)(2,1)} %get-tuple-element.8) | copy-start | bytes 1179652

commit v2 on v1

--- a/solution.py
+++ b/solution.py
@@ -36,14 +36,14 @@
 
 def kernel(
     nb, nt, positions,
-    trunk, gain, bias, scale, missing,
+    trunk, packed, missing,
     wq, wkv, wout, wup, skip, convw, headw, targets,
     pred, hgrad, fgrad,
     wq_v, wkv_v, wout_v, wup_v, conv_v, head_v, targ_v,
     skip_all, kv_all, q_v, acc_v, den_v, norm_v, hid_v, up_all, u32, win, xs, feat, slope,
-    part, part_in, hg, hg_in, hs, hs_in,
+    part, part_in, mid, hg, hg_in, hs, hs_in,
     load_sem, pred_sem,
-    skip_s, skip_r, kv1_s, kv1_r, kv2_s, kv2_r, kv3_s, kv3_r, up_s, up_r,
+    skip_s, skip_r, fwd_s, mid_s, mid_r, kv1_s, kv1_r, kv2_s, kv2_r, kv3_s, kv3_r, up_s, up_r,
     halo_s, halo_r, part_s, part_r, hg_s, hg_r, hs_s, hs_r,
 ):
     b, t = lax.axis_index("bin"), lax.axis_index("trk")
@@ -52,12 +52,15 @@
     heads = wq.shape[1] // dk
     npos, c2 = skip.shape
     tracks = headw.shape[1]
-    taps = convw.shape[0]
+    taps = convw.shape[0] // c2
     rim = taps // 2
     factor = npos // rows
     group = nt * npos
     half = nb // 2
     tile = 256
+    gain = packed.at[:, :chan]
+    bias = packed.at[:, chan:chan + tracks]
+    scale = packed.at[:, chan + tracks:]
 
     def send(src, dst, ssem, rsem, bb, tt):
         return pltpu.make_async_remote_copy(
@@ -84,11 +87,34 @@
     pl.semaphore_wait(barrier, len(greet))
 
     core = xor(b, 1, nb)
-    skip_c = [
-        send(skip, skip_all.at[t], skip_s.at[o], skip_r.at[o], b, xor(t, o, nt)) for o in range(1, nt)
-    ]
+    pair, todd, mate = lax.div(t, 2), lax.rem(t, 2), xor(t, 1, nt)
+
+    def far_side(j):
+        q = xor(pair, j, nt // 2)
+        up = jnp.where(q > pair, 1, 0)
+        return q, up, todd == up
+
+    skip_c = [send(skip, skip_all.at[t], skip_s.at[0], skip_r.at[1], b, mate)]
+    for j in range(1, nt // 2):
+        q, up, _ = far_side(j)
+        there = 2 * q + 1 - up
+        differ = todd + (1 - up) - 2 * todd * (1 - up)
+        skip_c.append(send(skip, skip_all.at[t], skip_s.at[j], skip_r.at[2 * j + differ], b, there))
     for copy in skip_c:
         copy.start()
+
+    def passed(o):
+        c = xor(t, o, nt)
+        return send(skip_all.at[c], skip_all.at[c], fwd_s.at[o], skip_r.at[xor(o, 1, nt)], b, mate)
+
+    def arrival(o):
+        return send(skip, skip_all.at[xor(t, o, nt)], skip_s.at[0], skip_r.at[o], b, mate)
+
+    def pass_on(o):
+        @pl.when(far_side(o // 2)[2])
+        def _():
+            arrival(o).wait_recv()
+            passed(o).start()
 
     wide = trunk[...].astype(F32)
     meansq = jnp.mean(wide * wide, axis=1, keepdims=True)
@@ -127,6 +153,8 @@
         copy.start()
         kv3.append(copy)
 
+    for o in range(2, nt, 2):
+        pass_on(o)
     acc_v[...] = jnp.zeros_like(acc_v)
     den_v[...] = jnp.zeros_like(den_v)
     score_scale = 1.0 / math.sqrt(dk)
@@ -153,6 +181,8 @@
     for copy in kv3:
         copy.wait_recv()
     lax.fori_loop(0, half, fold_core, 0)
+    for o in range(3, nt, 2):
+        pass_on(o)
 
     att = (acc_v[...] / jnp.sum(den_v[...], axis=1, keepdims=True)).astype(BF16)
     for h in range(heads):
@@ -174,8 +204,11 @@
         copy.start()
 
     loads[4].wait()
-    for copy in skip_c:
-        copy.wait_recv()
+    arrival(1).wait_recv()
+    for o in range(2, nt):
+        @pl.when(jnp.logical_not(far_side(o // 2)[2]))
+        def _():
+            arrival(o).wait_recv()
     for copy in ups:
         copy.wait_recv()
     spread = (
@@ -225,18 +258,27 @@
     for i in range(5, 8):
         loads[i].wait()
 
+    def is_near(o):
+        q = xor(pair, lax.div(o, 2), nt // 2)
+        return todd == jnp.where(q > pair, 1, 0)
+
+    def to_mate(o):
+        return send(part.at[o], mid.at[o], mid_s.at[o], mid_r.at[o], b, mate)
+
+    def to_owner(o):
+        j = lax.div(o, 2)
+        return send(part.at[o], part_in.at[j], part_s.at[o], part_r.at[j], b, xor(t, o, nt))
+
     def head_step(i, carry):
         o = nt - 1 - i
         c = xor(t, o, nt)
         base = pl.multiple_of(c * npos, npos)
         win[...] = u32[pl.ds(base, npos + 16), :]
         for k in range(taps):
-            xs[k] = win[8 + k - rim:8 + k - rim + npos, :].astype(BF16)
+            xs[:, k * c2:(k + 1) * c2] = win[8 + k - rim:8 + k - rim + npos, :].astype(BF16)
         for n in range(c2 // tile):
             cols = slice(n * tile, (n + 1) * tile)
-            acc = dot(xs[0], conv_v[0, :, cols])
-            for k in range(1, taps):
-                acc = acc + dot(xs[k], conv_v[k, :, cols])
+            acc = dot(xs[...], conv_v[:, cols])
             gelu = 0.5 * acc * (1.0 + jnp.tanh(math.sqrt(2.0 / math.pi) * (acc + 0.044715 * acc * acc * acc)))
             feat[pl.ds(base, npos), cols] = (
                 u32[pl.ds(pl.multiple_of(base + 8, 8), npos), cols] + gelu
@@ -273,9 +315,26 @@
                 g, head_v[cols, :], NT, preferred_element_type=F32
             ).astype(BF16)
 
-        @pl.when(o > 0)
-        def _():
-            send(part.at[o], part_in.at[o], part_s.at[o], part_r.at[o], b, c).start()
+        @pl.when(o == 1)
+        def _():
+            to_owner(o).start()
+
+        @pl.when(o >= 2)
+        def _():
+            @pl.when(jnp.logical_not(is_near(o)))
+            def _():
+                to_mate(o).start()
+
+        @pl.when(i >= 2)
+        def _():
+            late = nt + 1 - i
+
+            @pl.when(is_near(late))
+            def _():
+                to_mate(late).wait_recv()
+                z = xor(late, 1, nt)
+                part[z] = (part[z].astype(F32) + mid[late].astype(F32)).astype(BF16)
+                to_owner(z).start()
 
         return carry
 
@@ -315,13 +374,21 @@
     hgrad[...] = own
 
     total = part[0].astype(F32)
-    for o in range(1, nt):
-        send(part.at[o], part_in.at[o], part_s.at[o], part_r.at[o], b, xor(t, o, nt)).wait_recv()
-        total = total + part_in[o].astype(F32)
+    for j in range(nt // 2):
+        to_owner(max(2 * j, 1)).wait_recv()
+        total = total + part_in[j].astype(F32)
     fgrad[...] = total.astype(BF16)
 
-    for o in range(1, nt):
-        send(part.at[o], part_in.at[o], part_s.at[o], part_r.at[o], b, xor(t, o, nt)).wait_send()
+    to_owner(1).wait_send()
+    for o in range(2, nt):
+        @pl.when(far_side(o // 2)[2])
+        def _():
+            to_owner(o).wait_send()
+            passed(o).wait_send()
+
+        @pl.when(jnp.logical_not(far_side(o // 2)[2]))
+        def _():
+            to_mate(o).wait_send()
     for copy in skip_c + kv1 + kv2 + kv3 + ups + hgs + hss:
         copy.wait_send()
 
@@ -378,18 +445,18 @@
             jax.ShapeDtypeStruct((block, tracks), F32),
             jax.ShapeDtypeStruct((npos, c2), BF16),
         ),
-        in_specs=[vm] * 5 + [hbm] * 8,
+        in_specs=[vm] * 3 + [hbm] * 8,
         out_specs=(hbm, vm, vm),
         scratch_shapes=[
             V(w_query.shape, BF16), V(w_kv.shape, BF16), V(w_out.shape, BF16), V(w_up.shape, BF16),
-            V(conv_w.shape, BF16), V(head_w.shape, BF16), V((group, tracks), BF16),
+            V((taps * c2, c2), BF16), V(head_w.shape, BF16), V((group, tracks), BF16),
             V((nt, npos, c2), BF16), V((nb, nt, rows, 2 * dk), BF16), V((heads * rows, dk), BF16),
             V((heads * rows, dk), F32), V((heads * rows, dk), F32), V((rows, chan), BF16),
             V((rows, chan), BF16), V((nt, rows, c2), BF16), V((group + 16, c2), F32), V((npos + 16, c2), F32),
-            V((taps, npos, c2), BF16), V((group, c2), BF16), V((group, tracks), BF16),
-            V((nt, npos, c2), BF16), V((nt, npos, c2), BF16), V((c2, tracks), BF16),
+            V((npos, taps * c2), BF16), V((group, c2), BF16), V((group, tracks), BF16),
+            V((nt, npos, c2), BF16), V((nt // 2, npos, c2), BF16), V((nt, npos, c2), BF16), V((c2, tracks), BF16),
             V((half, block, tracks), BF16), V((half, block, tracks), BF16), V((half, block, tracks), BF16),
-            dma((8,)), dma((nt,)),
+            dma((8,)), dma((nt,)), dma((nt,)), dma((nt,)), dma((nt,)),
             dma((nt,)), dma((nt,)), dma((nt,)), dma((nt,)), dma((half,)), dma((half,)),
             dma((half,)), dma((half,)), dma((nt,)), dma((nt,)),
             dma((2,)), dma((2,)), dma((nt,)), dma((nt,)), dma((half,)), dma((half,)),
@@ -402,8 +469,8 @@
             flops=flops, bytes_accessed=24 * 1024 * 1024, transcendentals=4 * 1024 * 1024
         ),
     )(
-        trunk, norm_gain[None, :], head_bias[None, :], track_scale[None, :], missing[None, :],
-        w_query, w_kv, w_out, w_up, skip, conv_w, head_w, targets,
+        trunk, jnp.concatenate([norm_gain, head_bias, track_scale])[None, :], missing[None, :],
+        w_query, w_kv, w_out, w_up, skip, conv_w.reshape(taps * c2, c2), head_w, targets,
     )
 
 

time: 119 us -> 102 us (0.86)
  the two profiles are of different devices: /device:TPU:0 before, /device:TPU:14 now
where the time goes in v2:
time: 102 us; the launch traced here: 101 us
  Pallas kernels  92.5 us (91%)
  local copies, waits for them, and re-layouts  4.88 us (5%)
  other arithmetic  2.91 us (3%)
    pallas_call x1, Pallas kernels, body(): pl.pallas_call(functools.partial(kernel, nb, nt, float(group * nb)), out_...  92.5 us
    unnamed x7, local copies, waits for them, and re-layouts  4.18 us

profile of v2, /device:TPU:14, one launch (start us, length us, event | category | flops | bytes accessed | tf_op | source)
XLA Modules:
  0.0 101.0 jit_solution(2448431457918141131)
XLA Ops:
  0.6 0.8 convert_reduce_fusion
  1.5 0.7 multiply_divide_fusion
  2.1 0.7 dynamic-slice_reduce_fusion
  2.8 0.1 select_reduce_fusion
  2.9 1.3 %pad_maximum_fusion = f32[3072]{0:T(1024)} fusion(f32[768]{0:T(1024)S(1)} %select_reduce_fusion, f32[768]{0:T(1024)} %param.23, f32[1536]{0:T(1024)} %param.15), kind=kLoop, calls=%fused_computation.4 | loop fusion | flops 6144 | bytes 24576 | tf_op jit(solution)/shard_map/concatenate | solution.py:472
  4.3 92.5 %shard_map.157 = (bf16[1024,768]{1,0:T(8,128)(2,1)}, f32[96,768]{1,0:T(8,128)}, bf16[256,768]{1,0:T(8,128)(2,1)}) custom-call(bf16[64,1536]{1,0:T(8,128)(2,1)} %trunk.1, f32[1,3072]{1,0:T(1,128)} %bitcast.5, s32[1,256]{1,0:T(1,128)} %bitcast.7, bf16[1536,1024]{1,0:T(8,128)(2,1)} %wq.1, bf16[1536,256]{1,0:T(8,128)(2,1)} %wkv.1, bf16[1024,1536]{1,0:T(8,128)(2,1)} %wout.1, ...), custom_call_target="tpu_custom_call" | custom-call | flops 10804527104 | bytes 25165824 | tf_op jit(solution)/shard_map/pallas_call | solution.py:441
  96.8 0.0 copy-start.1
  96.8 0.0 copy-start
  96.8 2.7 %copy.20 = bf16[1024,768]{1,0:T(8,128)(2,1)} copy(bf16[1024,768]{1,0:T(8,128)(2,1)} %get-tuple-element.6) | data formatting | bytes 3145728
  99.5 0.0 copy-done.1
  99.5 0.7 copy.21
  100.2 0.0 copy-done
  100.2 0.7 copy.22
Async XLA Ops:
  96.8 2.7 %copy-start.1 = (f32[96,768]{1,0:T(8,128)S(1)}, f32[96,768]{1,0:T(8,128)}, u32[]{:S(2)}) copy-start(f32[96,768]{1,0:T(8,128)} %get-tuple-element.7) | copy-start | bytes 884740
  96.8 3.4 %copy-start = (bf16[256,768]{1,0:T(8,128)(2,1)S(1)}, bf16[256,768]{1,0:T(8,128)(2,1)}, u32[]{:S(2)}) copy-start(bf16[256,768]{1,0:T(8,128)(2,1)} %get-tuple-element.8) | copy-start | bytes 1179652

commit v3 on v2

--- a/solution.py
+++ b/solution.py
@@ -36,12 +36,12 @@
 
 def kernel(
     nb, nt, positions,
-    trunk, packed, missing,
+    trunk, gain, bias, missing, ids, weight,
     wq, wkv, wout, wup, skip, convw, headw, targets,
     pred, hgrad, fgrad,
     wq_v, wkv_v, wout_v, wup_v, conv_v, head_v, targ_v,
     skip_all, kv_all, q_v, acc_v, den_v, norm_v, hid_v, up_all, u32, win, xs, feat, slope,
-    part, part_in, mid, hg, hg_in, hs, hs_in,
+    bias_v, scale_v, part, part_in, mid, hg, hg_in, hs, hs_in,
     load_sem, pred_sem,
     skip_s, skip_r, fwd_s, mid_s, mid_r, kv1_s, kv1_r, kv2_s, kv2_r, kv3_s, kv3_r, up_s, up_r,
     halo_s, halo_r, part_s, part_r, hg_s, hg_r, hs_s, hs_r,
@@ -58,9 +58,6 @@
     group = nt * npos
     half = nb // 2
     tile = 256
-    gain = packed.at[:, :chan]
-    bias = packed.at[:, chan:chan + tracks]
-    scale = packed.at[:, chan + tracks:]
 
     def send(src, dst, ssem, rsem, bb, tt):
         return pltpu.make_async_remote_copy(
@@ -118,7 +115,7 @@
 
     wide = trunk[...].astype(F32)
     meansq = jnp.mean(wide * wide, axis=1, keepdims=True)
-    norm_v[...] = (wide * lax.rsqrt(meansq + 1e-06) * gain[...]).astype(BF16)
+    norm_v[...] = (wide * lax.rsqrt(meansq + 1e-06) * gain[...].reshape(1, chan)).astype(BF16)
     loads[0].wait()
     kv_all[b, t] = dot(norm_v[...], wkv_v[...]).astype(BF16)
     kv1 = [
@@ -135,6 +132,16 @@
         for k in range(per):
             h = i * per + k
             q_v[h * rows:(h + 1) * rows, :] = res[:, k * dk:(k + 1) * dk]
+
+    bias_v[...] = bias[...].reshape(1, tracks)
+    total_tracks = ids.shape[1]
+    groups = weight.shape[0]
+    local = ids[:, pl.ds(pl.multiple_of(t * tracks, tracks), tracks)]
+    track_scale = jnp.zeros((1, tracks), F32)
+    for g in range(groups):
+        count = jnp.sum((ids[...] == g).astype(F32), axis=1, keepdims=True)
+        track_scale = jnp.where(local == g, weight[g] * total_tracks / (groups * count), track_scale)
+    scale_v[...] = track_scale
 
     for copy in kv1:
         copy.wait_recv()
@@ -296,14 +303,14 @@
         keep = jnp.concatenate([keep] * (tile // 128), axis=1)
         for n in range(tracks // tile):
             cols = slice(n * tile, (n + 1) * tile)
-            x = dot(f, head_v[:, cols]) + bias[:, cols]
+            x = dot(f, head_v[:, cols]) + bias_v[:, cols]
             e = jnp.exp(-jnp.abs(x))
             u = 1.0 + e
             r = 1.0 / u
             smooth = jnp.maximum(x, 0.0) + (jnp.log(u) + (e - (u - 1.0)) * r)
             sig = jnp.where(x >= 0, r, e * r)
             misfit = smooth - targ_v[pl.ds(base, npos), cols].astype(F32)
-            slope[pl.ds(base, npos), cols] = (keep * scale[:, cols] * misfit * sig).astype(BF16)
+            slope[pl.ds(base, npos), cols] = (keep * scale_v[:, cols] * misfit * sig).astype(BF16)
             targ_v[pl.ds(base, npos), cols] = smooth.astype(BF16)
         pltpu.make_async_copy(
             targ_v.at[pl.ds(base, npos)], pred.at[pl.ds(base, npos)], pred_sem.at[i]
@@ -341,35 +348,45 @@
     lax.fori_loop(0, nt, head_step, 0)
 
     block = c2 // nb
+    mine = lax.div(b, 2)
+    odd = lax.rem(b, 2)
+
+    def to_core(j):
+        row = pl.multiple_of((2 * j + 1 - odd) * block, block)
+        return send(hg.at[pl.ds(row, block)], hg_in.at[j], hg_s.at[j], hg_r.at[j], core, t)
+
+    def to_chip(j):
+        return send(
+            hs.at[j], hs_in.at[xor(mine, j, half)], hs_s.at[j], hs_r.at[xor(mine, j, half)], 2 * j + odd, t
+        )
+
+    def chip_sum(j):
+        to_core(j).wait_recv()
+        row = pl.multiple_of((2 * j + odd) * block, block)
+        hs[j] = (hg[pl.ds(row, block), :].astype(F32) + hg_in[j].astype(F32)).astype(BF16)
+
+        @pl.when(mine != j)
+        def _():
+            to_chip(j).start()
+
+    sent = summed = 0
     for n in range(c2 // tile):
         rws = slice(n * tile, (n + 1) * tile)
-        for m in range(tracks // tile):
-            cols = slice(m * tile, (m + 1) * tile)
-            hg[rws, cols] = (
-                lax.dot_general(feat[:, rws], slope[:, cols], TN, preferred_element_type=F32)
-                * (1.0 / positions)
-            ).astype(BF16)
-    mine = lax.div(b, 2)
-    odd = lax.rem(b, 2)
-    hgs = []
-    for j in range(half):
-        row = pl.multiple_of((2 * j + 1 - odd) * block, block)
-        copy = send(hg.at[pl.ds(row, block)], hg_in.at[j], hg_s.at[j], hg_r.at[j], core, t)
-        copy.start()
-        hgs.append(copy)
-    for copy in hgs:
-        copy.wait_recv()
-    hss = []
+        hg[rws, :] = (
+            lax.dot_general(feat[:, rws], slope[...], TN, preferred_element_type=F32) * (1.0 / positions)
+        ).astype(BF16)
+        while summed < sent:
+            chip_sum(summed)
+            summed += 1
+        while sent < half and (2 * sent + 2) * block <= (n + 1) * tile:
+            to_core(sent).start()
+            sent += 1
+    while summed < half:
+        chip_sum(summed)
+        summed += 1
+    own = hs[mine].astype(F32)
     for j in range(1, half):
-        q = xor(b, 2 * j, nb)
-        row = pl.multiple_of(q * block, block)
-        hs[j] = (hg[pl.ds(row, block), :].astype(F32) + hg_in[lax.div(q, 2)].astype(F32)).astype(BF16)
-        copy = send(hs.at[j], hs_in.at[j], hs_s.at[j], hs_r.at[j], q, t)
-        copy.start()
-        hss.append(copy)
-    own = hg[pl.ds(pl.multiple_of(b * block, block), block), :].astype(F32) + hg_in[mine].astype(F32)
-    for j in range(1, half):
-        hss[j - 1].wait_recv()
+        send(hs.at[0], hs_in.at[j], hs_s.at[0], hs_r.at[j], core, t).wait_recv()
         own = own + hs_in[j].astype(F32)
     hgrad[...] = own
 
@@ -389,8 +406,14 @@
         @pl.when(jnp.logical_not(far_side(o // 2)[2]))
         def _():
             to_mate(o).wait_send()
-    for copy in skip_c + kv1 + kv2 + kv3 + ups + hgs + hss:
+    for copy in skip_c + kv1 + kv2 + kv3 + ups:
         copy.wait_send()
+    for j in range(half):
+        to_core(j).wait_send()
+
+        @pl.when(mine != j)
+        def _():
+            to_chip(j).wait_send()
 
     @pl.when(b < nb - 1)
     def _():
@@ -421,14 +444,6 @@
     group = nt * npos
     half = nb // 2
     block = c2 // nb
-
-    groups = group_weight.shape[0]
-    total_tracks = group_ids.shape[0]
-    labels = jnp.arange(groups, dtype=jnp.int32)
-    counts = jnp.sum((group_ids == labels[None, :]).astype(jnp.int32), axis=0)
-    per_group = group_weight * total_tracks / (groups * counts.astype(F32))
-    local_ids = lax.dynamic_slice_in_dim(group_ids, lax.axis_index("trk") * tracks, tracks, 0)
-    track_scale = jnp.sum(jnp.where(local_ids == labels[None, :], per_group[None, :], 0.0), axis=1)
 
     vm = pl.BlockSpec(memory_space=pltpu.VMEM)
     hbm = pl.BlockSpec(memory_space=pl.ANY)
@@ -445,7 +460,7 @@
             jax.ShapeDtypeStruct((block, tracks), F32),
             jax.ShapeDtypeStruct((npos, c2), BF16),
         ),
-        in_specs=[vm] * 3 + [hbm] * 8,
+        in_specs=[vm] * 5 + [pl.BlockSpec(memory_space=pltpu.SMEM)] + [hbm] * 8,
         out_specs=(hbm, vm, vm),
         scratch_shapes=[
             V(w_query.shape, BF16), V(w_kv.shape, BF16), V(w_out.shape, BF16), V(w_up.shape, BF16),
@@ -454,6 +469,7 @@
             V((heads * rows, dk), F32), V((heads * rows, dk), F32), V((rows, chan), BF16),
             V((rows, chan), BF16), V((nt, rows, c2), BF16), V((group + 16, c2), F32), V((npos + 16, c2), F32),
             V((npos, taps * c2), BF16), V((group, c2), BF16), V((group, tracks), BF16),
+            V((1, tracks), F32), V((1, tracks), F32),
             V((nt, npos, c2), BF16), V((nt // 2, npos, c2), BF16), V((nt, npos, c2), BF16), V((c2, tracks), BF16),
             V((half, block, tracks), BF16), V((half, block, tracks), BF16), V((half, block, tracks), BF16),
             dma((8,)), dma((nt,)), dma((nt,)), dma((nt,)), dma((nt,)),
@@ -469,7 +485,7 @@
             flops=flops, bytes_accessed=24 * 1024 * 1024, transcendentals=4 * 1024 * 1024
         ),
     )(
-        trunk, jnp.concatenate([norm_gain, head_bias, track_scale])[None, :], missing[None, :],
+        trunk, norm_gain, head_bias, missing[None, :], group_ids.reshape(1, -1), group_weight,
         w_query, w_kv, w_out, w_up, skip, conv_w.reshape(taps * c2, c2), head_w, targets,
     )
 

time: 102 us -> 100 us (0.980)
  other arithmetic: 2.91 us -> 0 us
  Pallas kernels: 92.5 us -> 95.1 us
    pallas_call x1, Pallas kernels: 92.5 us -> 95.1 us  [body(): pl.pallas_call(functools.partial(kernel, nb, nt, float(group * nb)), out_...]
    concatenate x1 -> x0, other arithmetic: 1.32 us -> none  [body(): jnp.concatenate([norm_gain, head_bias, track_scale])[None, :]]
where the time goes in v3:
time: 100 us; the launch traced here: 99.9 us
  Pallas kernels  95.1 us (95%)
  local copies, waits for them, and re-layouts  4.18 us (4%)
    pallas_call x1, Pallas kernels, body(): pl.pallas_call(functools.partial(kernel, nb, nt, float(group * nb)), out_...  95.1 us
    unnamed x7, local copies, waits for them, and re-layouts  4.18 us

profile of v3, /device:TPU:14, one launch (start us, length us, event | category | flops | bytes accessed | tf_op | source)
XLA Modules:
  0.0 99.9 jit_solution(11827031096529668749)
XLA Ops:
  0.6 95.1 %shard_map.157 = (bf16[1024,768]{1,0:T(8,128)(2,1)}, f32[96,768]{1,0:T(8,128)}, bf16[256,768]{1,0:T(8,128)(2,1)}) custom-call(bf16[64,1536]{1,0:T(8,128)(2,1)} %trunk.1, f32[1536]{0:T(1024)} %gain.1, f32[768]{0:T(1024)} %bias.1, s32[1,256]{1,0:T(1,128)} %bitcast.5, s32[1,3072]{1,0:T(1,128)} %bitcast.4, f32[11]{0:T(128)} %weight.1, bf16[1536,1024]{1,0:T(8,128)(2,1)} %wq.1, ...), custom_call_target="tpu_custom_call" | custom-call | flops 10804527104 | bytes 25165824 | tf_op jit(solution)/shard_map/pallas_call | solution.py:456
  95.7 0.0 copy-start.1
  95.7 0.0 copy-start
  95.7 2.7 %copy.20 = bf16[1024,768]{1,0:T(8,128)(2,1)} copy(bf16[1024,768]{1,0:T(8,128)(2,1)} %get-tuple-element.6) | data formatting | bytes 3145728
  98.5 0.0 copy-done.1
  98.5 0.7 copy.21
  99.2 0.0 copy-done
  99.2 0.7 copy.22
Async XLA Ops:
  95.7 2.7 %copy-start.1 = (f32[96,768]{1,0:T(8,128)S(1)}, f32[96,768]{1,0:T(8,128)}, u32[]{:S(2)}) copy-start(f32[96,768]{1,0:T(8,128)} %get-tuple-element.7) | copy-start | bytes 884740
  95.7 3.4 %copy-start = (bf16[256,768]{1,0:T(8,128)(2,1)S(1)}, bf16[256,768]{1,0:T(8,128)(2,1)}, u32[]{:S(2)}) copy-start(bf16[256,768]{1,0:T(8,128)(2,1)} %get-tuple-element.8) | copy-start | bytes 1179652

commit v4 on v3

--- a/solution.py
+++ b/solution.py
@@ -185,11 +185,11 @@
         return carry
 
     lax.fori_loop(0, half, fold_own, 0)
+    for o in range(3, nt, 2):
+        pass_on(o)
     for copy in kv3:
         copy.wait_recv()
     lax.fori_loop(0, half, fold_core, 0)
-    for o in range(3, nt, 2):
-        pass_on(o)
 
     att = (acc_v[...] / jnp.sum(den_v[...], axis=1, keepdims=True)).astype(BF16)
     for h in range(heads):

time: 100 us -> 100 us (level)
  no operation moved by 1% of the time
where the time goes in v4:
time: 100 us; the launch traced here: 99.9 us
  Pallas kernels  95.1 us (95%)
  local copies, waits for them, and re-layouts  4.18 us (4%)
    pallas_call x1, Pallas kernels, body(): pl.pallas_call(functools.partial(kernel, nb, nt, float(group * nb)), out_...  95.1 us
    unnamed x7, local copies, waits for them, and re-layouts  4.18 us

profile of v4, /device:TPU:14, one launch (start us, length us, event | category | flops | bytes accessed | tf_op | source)
XLA Modules:
  0.0 99.9 jit_solution(3892166915488595462)
XLA Ops:
  0.6 95.1 %shard_map.157 = (bf16[1024,768]{1,0:T(8,128)(2,1)}, f32[96,768]{1,0:T(8,128)}, bf16[256,768]{1,0:T(8,128)(2,1)}) custom-call(bf16[64,1536]{1,0:T(8,128)(2,1)} %trunk.1, f32[1536]{0:T(1024)} %gain.1, f32[768]{0:T(1024)} %bias.1, s32[1,256]{1,0:T(1,128)} %bitcast.5, s32[1,3072]{1,0:T(1,128)} %bitcast.4, f32[11]{0:T(128)} %weight.1, bf16[1536,1024]{1,0:T(8,128)(2,1)} %wq.1, ...), custom_call_target="tpu_custom_call" | custom-call | flops 10804527104 | bytes 25165824 | tf_op jit(solution)/shard_map/pallas_call | solution.py:456
  95.7 0.0 copy-start.1
  95.7 0.0 copy-start
  95.7 2.7 %copy.20 = bf16[1024,768]{1,0:T(8,128)(2,1)} copy(bf16[1024,768]{1,0:T(8,128)(2,1)} %get-tuple-element.6) | data formatting | bytes 3145728
  98.5 0.0 copy-done.1
  98.5 0.7 copy.21
  99.2 0.0 copy-done
  99.2 0.7 copy.22
Async XLA Ops:
  95.7 2.7 %copy-start.1 = (f32[96,768]{1,0:T(8,128)S(1)}, f32[96,768]{1,0:T(8,128)}, u32[]{:S(2)}) copy-start(f32[96,768]{1,0:T(8,128)} %get-tuple-element.7) | copy-start | bytes 884740
  95.7 3.4 %copy-start = (bf16[256,768]{1,0:T(8,128)(2,1)S(1)}, bf16[256,768]{1,0:T(8,128)(2,1)}, u32[]{:S(2)}) copy-start(bf16[256,768]{1,0:T(8,128)(2,1)} %get-tuple-element.8) | copy-start | bytes 1179652
